TPU v7x, 32 devices: a whole 2x2x4 slice. The times are simulated.
32 devices in a mesh: groups: 2 (over x), rep: 16 (over z, y, core).
Axes of the slice: x: 2, y: 2, z: 4, core: 2. Of those that a mesh axis runs over, the one named last changes fastest.
Arguments:
- tokens: bfloat16 [4096, 4096], P(('groups', 'rep')), parts along dimension 0, may hold values from -6 to 6
- cotangent: bfloat16 [4096, 11008], P(('groups', 'rep')), parts along dimension 0, may hold values from -0.4375 to 0.4375
- basis: bfloat16 [4096, 1024], P('rep'), may hold values from -0.09375 to 0.09375
- moment: float32 [1024, 11008], P(None, 'rep'), may hold values from -1.5 to 1.5
- second_moment: float32 [1024, 11008], P(None, 'rep'), may hold values from 0.002 to 0.05
Outputs:
- update: bfloat16 [8192, 11008], P(('groups', 'rep')), parts along dimension 0
- moment_next: float32 [2048, 11008], P('groups', 'rep'), parts along dimension 0
- second_next: float32 [2048, 11008], P('groups', 'rep'), parts along dimension 0
There are 2 independent parts, one for each index of `groups`. A program takes and returns all parts, laid end to end along the dimension named above; an argument that names none is the same for every part. Nothing has to cross between parts.
All inputs are finite; a program needn't handle non-finite values.
Results may differ from a plain program's by a relative error of at most 0.0055.
Values may be sent and summed in bfloat16 or wider, within the bound.
A program may use at most 128 MiB of HBM per device.

v0:
```python
import jax
import jax.numpy as jnp
from jax import lax
from jax.sharding import PartitionSpec as P


def adam_part(low_grad, moment, second_moment):
    moment_next = 0.9 * moment + 0.1 * low_grad
    second_next = 0.999 * second_moment + 0.001 * low_grad * low_grad
    ratio = (moment_next / (jnp.sqrt(second_next) + 1e-08)).astype(jnp.bfloat16)
    return (moment_next, second_next, ratio)


def on_device(tokens, cotangent, basis, moment, second_moment):
    full_basis = lax.all_gather(basis, "rep", axis=0, tiled=True)
    projected = jnp.dot(tokens, full_basis, preferred_element_type=jnp.float32).astype(jnp.bfloat16)
    columns = lax.all_to_all(cotangent, "rep", split_axis=1, concat_axis=0, tiled=True)
    low_grad = lax.dot_general(
        lax.all_gather(projected, "rep", axis=0, tiled=True),
        columns,
        (((0,), (0,)), ((), ())),
        preferred_element_type=jnp.float32,
    )
    moment_next, second_next, ratio = adam_part(low_grad, moment, second_moment)
    expanded = jnp.dot(full_basis, ratio, preferred_element_type=jnp.float32)
    update_columns = expanded.astype(jnp.bfloat16)
    update = lax.all_to_all(update_columns, "rep", split_axis=0, concat_axis=1, tiled=True)
    return (update, moment_next, second_next)


def solution(mesh):
    in_specs = (
        P(("groups", "rep"), None),
        P(("groups", "rep"), None),
        P("rep", None),
        P(None, "rep"),
        P(None, "rep"),
    )
    out_specs = (P(("groups", "rep"), None), P("groups", "rep"), P("groups", "rep"))
    return jax.shard_map(
        on_device, mesh=mesh, in_specs=in_specs, out_specs=out_specs, check_vma=False
    )
```

profile of v0, /device:TPU:1, one launch (start us, length us, event | category | flops | bytes accessed | tf_op | source)
XLA Modules:
  0.0 352.6 jit_solution(14673022090579044792)
XLA Ops:
  7.2 0.0 copy-start
  7.2 0.0 all-gather.3.cloned.1.call-start
  7.2 0.7 all-gather.3.cloned.1.call-update
  7.9 0.0 all-gather.5.cloned.1.call-start
  8.0 79.7 %all-gather.3.cloned.1.call-done = bf16[4096,1024]{1,0:T(8,128)(2,1)} async-done(((bf16[256,1024]{1,0:T(8,128)(2,1)}), bf16[4096,1024]{1,0:T(8,128)(2,1)}) %all-gather.3.cloned.1.call-update) | async-done | bytes 8388624 | tf_op jit(solution)/shard_map/all_gather | solution.py:15
  87.6 0.0 copy-done
  87.6 5.3 %convolution_convert_fusion.1 = bf16[128,1024]{1,0:T(8,128)(2,1)} fusion(bf16[128,4096]{1,0:T(8,128)(2,1)S(1)} %copy-done, bf16[4096,1024]{1,0:T(8,128)(2,1)} %all-gather.3.cloned.1.call-done), kind=kOutput, calls=%fused_computation.10 | convolution fusion | flops 1073872896 | bytes 9699328 | tf_op jit(solution)/shard_map/dot_general | solution.py:16
  93.0 0.0 all-gather.5.cloned.1.call-update
  93.0 4.5 %copy.9 = bf16[128,11008]{0,1:T(8,128)(2,1)} copy(bf16[128,11008]{1,0:T(8,128)(2,1)} %param.6) | data formatting | bytes 5636096 | tf_op args[1]
  97.5 91.7 %all_to_all.38 = bf16[128,16,688]{0,2,1:T(8,128)(2,1)} all-to-all(bf16[128,16,688]{0,2,1:T(8,128)(2,1)} %bitcast.25), channel_id=1, replica_groups=mesh['groups'=2,'rep'=16] {'rep'}, dimensions={1} | all-to-all | bytes 5636096 | tf_op jit(solution)/shard_map/all_to_all | solution.py:17
  189.1 0.0 all-gather.5.cloned.1.call-done
  189.1 8.2 %fusion = (f32[1024,688]{0,1:T(8,128)S(1)}, f32[1024,688]{0,1:T(8,128)S(1)}) fusion(f32[1024,688]{0,1:T(8,128)} %param.9, f32[1024,688]{0,1:T(8,128)} %param.8, bf16[2048,1024]{1,0:T(8,128)(2,1)} %all-gather.5.cloned.1.call-done, bf16[128,16,688]{0,2,1:T(8,128)(2,1)} %all_to_all.38), kind=kOutput, calls=%fused_computation.3 | convolution fusion | flops 2890612736 | bytes 18284544 | tf_op jit(solution)/shard_map/dot_general | solution.py:18
  197.3 0.0 copy-start.1
  197.3 0.0 copy-start.2
  197.4 12.0 %convolution_convert_fusion = bf16[688,4096]{1,0:T(8,128)(2,1)S(1)} fusion(bf16[4096,1024]{1,0:T(8,128)(2,1)} %all-gather.3.cloned.1.call-done, f32[1024,688]{0,1:T(8,128)S(1)} %get-tuple-element.7, f32[1024,688]{0,1:T(8,128)S(1)} %get-tuple-element.6), kind=kOutput, calls=%fused_computation | convolution fusion | flops 5776293888 | bytes 19660800 | tf_op jit(solution)/shard_map/dot_general | solution.py:25
  209.3 0.0 copy-done.1
  209.3 0.0 copy-done.2
  209.3 0.4 copy.22
  209.7 127.7 %all_to_all.39 = bf16[16,256,688]{1,2,0:T(8,128)(2,1)} all-to-all(bf16[16,256,688]{1,2,0:T(8,128)(2,1)S(1)} %bitcast.23), channel_id=1, replica_groups=mesh['groups'=2,'rep'=16] {'rep'}, dimensions={0} | all-to-all | bytes 11272192 | tf_op jit(solution)/shard_map/all_to_all | solution.py:27
  337.4 8.3 %copy.12 = bf16[256,11008]{1,0:T(8,128)(2,1)} copy(bf16[256,11008]{0,1:T(8,128)(2,1)} %bitcast.24) | data formatting | bytes 11272192
Async XLA Ops:
  7.2 80.5 %copy-start = (bf16[128,4096]{1,0:T(8,128)(2,1)S(1)}, bf16[128,4096]{1,0:T(8,128)(2,1)}, u32[]{:S(2)}) copy-start(bf16[128,4096]{1,0:T(8,128)(2,1)} %param.5) | copy-start | bytes 3145732
  7.2 80.4 %all-gather.3.cloned.1.call-start = ((), (), s32[]{:S(2)}) async-start(), calls=%async_computation.2 | async-start | bytes 8912896 | tf_op jit(solution)/shard_map/all_gather | solution.py:15
  7.9 181.2 %all-gather.5.cloned.1.call-start = ((), (), s32[]{:S(2)}) async-start(), calls=%async_computation.3 | async-start | bytes 4456448 | tf_op jit(solution)/shard_map/all_gather | solution.py:19
  197.3 12.0 %copy-start.1 = (f32[1024,688]{0,1:T(8,128)}, f32[1024,688]{0,1:T(8,128)S(1)}, u32[]{:S(2)}) copy-start(f32[1024,688]{0,1:T(8,128)S(1)} %get-tuple-element.6) | copy-start | bytes 8454148
  197.3 12.0 %copy-start.2 = (f32[1024,688]{0,1:T(8,128)}, f32[1024,688]{0,1:T(8,128)S(1)}, u32[]{:S(2)}) copy-start(f32[1024,688]{0,1:T(8,128)S(1)} %get-tuple-element.7) | copy-start | bytes 8454148
Sparse Core Ops, SparseCore 0:
  10.2 77.3 all-gather.2
  93.1 79.2 all-gather.4
where the time goes:
time: 353 us
  blocking collectives  219 us (62%)
  waiting for transfers between devices  80.4 us (23%)
  matrix products  25.5 us (7%)
  between operations  14.1 us (4%)
  local copies, waits for them, and re-layouts  13.2 us (4%)
    all_to_all x1, blocking collectives, on_device(): lax.all_to_all(update_columns, 'rep', split_axis=0, concat_axis=1, tiled=...  128 us
    all_to_all x1, blocking collectives, on_device(): lax.all_to_all(cotangent, 'rep', split_axis=1, concat_axis=0, tiled=True)  91.7 us
    all_gather x1, waiting for transfers between devices, on_device(): full_basis = lax.all_gather(basis, 'rep', axis=0, tiled=True)  79.7 us
    unnamed x8, local copies, waits for them, and re-layouts  12.8 us
    dot_general x1, matrix products, on_device(): expanded = jnp.dot(full_basis, ratio, preferred_element_type=jnp.float32)  12 us
    dot_general x1, matrix products, on_device(): lax.dot_general(lax.all_gather(projected, 'rep', axis=0, tiled=True), col...  8.18 us
  transfers between devices with their start and end apart: 2, of which 1 were waited for; matrix products, arithmetic and copies ran while one was open for 1% of the time, Pallas kernels for 0%

commit v1 on v0

v1 whole, which is shorter than its diff:
```python
import functools

import jax
import jax.numpy as jnp
from jax import lax
from jax.experimental import pallas as pl
from jax.experimental.pallas import tpu as pltpu
from jax.sharding import PartitionSpec as P

CORES = 2
NT = (((1,), (1,)), ((), ()))


def kernel(
    n, Z, Y, tokens_hbm, ct_hbm, basis_hbm, moment_hbm, second_hbm,
    out_hbm, moment_out, second_out,
    tok, ball, pacc, ptall, ctall, mom, sec, rt, ubuf,
    lsem, asem, bsem, psem, csem_s, csem_r, usem_s, usem_r, rsem,
):
    me = lax.axis_index("rep")
    z = me // (Y * CORES)
    y = (me // CORES) % Y
    c = me % CORES
    rows = basis_hbm.shape[0]
    T = tokens_hbm.shape[0]
    rank = basis_hbm.shape[1]

    def dev(zz, yy, cc):
        return (zz * Y + yy) * CORES + cc

    barrier = pltpu.get_barrier_semaphore()

    @pl.loop(1, n)
    def _(k):
        pl.semaphore_signal(
            barrier, inc=1, device_id={"rep": (me + k) % n},
            device_id_type=pl.DeviceIdType.MESH,
        )

    def local(src, dst, i):
        return pltpu.make_async_copy(src, dst, lsem.at[i])

    def remote(src, dst, ss, rs, to):
        return pltpu.make_async_remote_copy(
            src_ref=src, dst_ref=dst, send_sem=ss, recv_sem=rs,
            device_id={"rep": to}, device_id_type=pl.DeviceIdType.MESH,
        )

    def bas(b):
        return ball.at[pl.ds(pl.multiple_of(b * rows, 16), rows), :]

    def pro(b):
        return ptall.at[:, pl.ds(pl.multiple_of(b * T, 128), T)]

    def cot(b):
        return ctall.at[:, pl.ds(pl.multiple_of(b * T, 128), T)]

    own = local(basis_hbm, bas(me), 0)
    own.start()
    load_tok = local(tokens_hbm, tok, 1)
    load_tok.start()
    load_mom = local(moment_hbm, mom, 2)
    load_mom.start()
    load_sec = local(second_hbm, sec, 3)
    load_sec.start()
    own_ct = local(ct_hbm.at[me], cot(me), 4)
    own_ct.start()
    own.wait()
    pl.semaphore_wait(barrier, n - 1)

    def up(blk, S, zs):
        b = blk(dev(zs, y, c))
        return remote(b, b, S.at[0, zs], S.at[5, zs], dev((z + 1) % Z, y, c))

    def down(blk, S, zs):
        b = blk(dev(zs, y, c))
        return remote(b, b, S.at[1, zs], S.at[5, zs], dev((z + Z - 1) % Z, y, c))

    def across(blk, S, zs, recv=False):
        b = blk(dev(zs, (y + 1) % Y if recv else y, c))
        return remote(b, b, S.at[2, zs], S.at[6, zs], dev(z, (y + 1) % Y, c))

    def core(blk, S, zs, ys, recv=False):
        b = blk(dev(zs, ys, (c + 1) % CORES if recv else c))
        i = (ys + Y - y) % Y
        return remote(b, b, S.at[3 + i, zs], S.at[7 + ys, zs], dev(z, y, (c + 1) % CORES))

    def spread(blk, S, zs):
        if Y > 1:
            across(blk, S, zs).start()
        core(blk, S, zs, y).start()

    def both(k, f):
        @pl.when(z - k >= 0)
        def _():
            f(z - k, True)

        @pl.when(z + k < Z)
        def _():
            f(z + k, False)

    def line_start(blk, S):
        @pl.when(z + 1 < Z)
        def _():
            up(blk, S, z).start()

        @pl.when(z >= 1)
        def _():
            down(blk, S, z).start()

    def line_take(blk, S, zs, below):
        up(blk, S, zs).wait_recv()
        if below:
            @pl.when(z + 1 < Z)
            def _():
                up(blk, S, zs).start()
        else:
            @pl.when(z >= 1)
            def _():
                down(blk, S, zs).start()

    def line_sent(blk, S):
        @pl.loop(0, Z)
        def _(zs):
            @pl.when((zs <= z) & (z + 1 < Z))
            def _():
                up(blk, S, zs).wait_send()

            @pl.when((zs >= z) & (z >= 1))
            def _():
                down(blk, S, zs).wait_send()

    def gather(blk, S, middle=None):
        def crossed(zs, _=None):
            if Y > 1:
                across(blk, S, zs, recv=True).wait_recv()
                core(blk, S, zs, (y + 1) % Y).start()

        def arrived(zs, below):
            line_take(blk, S, zs, below)
            spread(blk, S, zs)

        line_start(blk, S)
        spread(blk, S, z)

        @pl.loop(1, Z)
        def _(k):
            both(k, arrived)

            @pl.when(k == 1)
            def _():
                crossed(z)

            @pl.when(k > 1)
            def _():
                both(k - 1, crossed)

        if middle is not None:
            middle()
        both(Z - 1, crossed)

        @pl.loop(0, Z)
        def _(zs):
            for ys in range(Y):
                core(blk, S, zs, ys, recv=True).wait_recv()

    def gather_sent(blk, S):
        line_sent(blk, S)

        @pl.loop(0, Z)
        def _(zs):
            if Y > 1:
                across(blk, S, zs).wait_send()
            for ys in range(Y):
                core(blk, S, zs, ys).wait_send()

    def cot_copy(k):
        to = (me + k) % n
        return remote(ct_hbm.at[to], cot(me), csem_s.at[k], csem_r.at[me], to)

    def cot_start():
        @pl.loop(1, n)
        def _(k):
            cot_copy(k).start()

    gather(bas, bsem, cot_start)

    load_tok.wait()
    pacc[...] = jnp.zeros_like(pacc)
    step = 512

    @pl.loop(0, ball.shape[0] // step)
    def _(k):
        at = pl.ds(pl.multiple_of(k * step, step), step)
        pacc[...] += jnp.dot(tok[:, at], ball[at, :], preferred_element_type=jnp.float32)

    pro(me)[...] = pacc[...].T.astype(jnp.bfloat16)
    gather(pro, psem)

    @pl.loop(1, n)
    def _(k):
        src = (me + k) % n
        remote(cot(src), cot(src), csem_s.at[k], csem_r.at[src], src).wait_recv()

    own_ct.wait()
    load_mom.wait()
    load_sec.wait()

    def adam_copy(i, r):
        src, dst = ((mom, moment_out), (sec, second_out))[i]
        at = pl.ds(pl.multiple_of(r * 128, 128), 128)
        return pltpu.make_async_copy(src.at[at, :], dst.at[at, :], asem.at[i, r])

    @pl.loop(0, rank // 128)
    def _(r):
        at = pl.ds(pl.multiple_of(r * 128, 128), 128)
        low = lax.dot_general(ptall[at, :], ctall[...], NT, preferred_element_type=jnp.float32)
        moment_next = 0.9 * mom[at, :] + 0.1 * low
        second_next = 0.999 * sec[at, :] + 0.001 * low * low
        mom[at, :] = moment_next
        sec[at, :] = second_next
        ratio = moment_next / (jnp.sqrt(second_next) + 1e-08)
        rt[z, :, at] = ratio.T.astype(jnp.bfloat16)
        adam_copy(0, r).start()
        adam_copy(1, r).start()

    def rat(b):
        return rt.at[b // (Y * CORES)]

    planes = Y * CORES

    def u_copy(p, zs, recv=False):
        b = dev(zs, 0, 0) + (p if recv else me % planes)
        src = ubuf.at[p, zs]
        return remote(src, out_hbm.at[b], usem_s.at[p, zs], usem_r.at[p if recv else me % planes, zs], z * planes + p)

    def u_local(zs):
        q = me % planes
        return pltpu.make_async_copy(ubuf.at[q, zs], out_hbm.at[dev(zs, y, c)], usem_s.at[q, zs])

    def expand(zs):
        for i in range(planes):
            p = (me + i + 1) % planes
            at = pl.ds(pl.multiple_of((z * planes + p) * rows, 16), rows)
            ubuf[p, zs] = lax.dot_general(
                ball[at, :], rt[zs], NT, preferred_element_type=jnp.float32
            ).astype(jnp.bfloat16)
            if i < planes - 1:
                u_copy(p, zs).start()
            else:
                u_local(zs).start()

    def ratio_arrived(zs, below):
        line_take(rat, rsem, zs, below)
        expand(zs)

    line_start(rat, rsem)
    expand(z)

    @pl.loop(1, Z)
    def _(k):
        both(k, ratio_arrived)

    gather_sent(bas, bsem)
    gather_sent(pro, psem)
    line_sent(rat, rsem)

    @pl.loop(1, n)
    def _(k):
        cot_copy(k).wait_send()

    @pl.loop(0, rank // 128)
    def _(r):
        adam_copy(0, r).wait()
        adam_copy(1, r).wait()

    @pl.loop(0, Z)
    def _(zs):
        for i in range(1, planes):
            p = (me + i) % planes
            u_copy(p, zs).wait_send()
            u_copy(p, zs, recv=True).wait_recv()
        u_local(zs).wait()


def on_device(n, Z, Y, tokens, cotangent, basis, moment, second_moment):
    T, D = tokens.shape
    rows, rank = basis.shape
    width = moment.shape[1]
    bf = jnp.bfloat16
    ct = cotangent.T.reshape(n, width, T)
    any_spec = pl.BlockSpec(memory_space=pl.ANY)
    dma = pltpu.SemaphoreType.DMA
    out, moment_next, second_next = pl.pallas_call(
        functools.partial(kernel, n, Z, Y),
        out_shape=(
            jax.ShapeDtypeStruct((n, rows, width), bf),
            jax.ShapeDtypeStruct(moment.shape, jnp.float32),
            jax.ShapeDtypeStruct(moment.shape, jnp.float32),
        ),
        in_specs=[any_spec] * 5,
        out_specs=(any_spec,) * 3,
        scratch_shapes=[
            pltpu.VMEM((T, D), bf),
            pltpu.VMEM((D, rank), bf),
            pltpu.VMEM((T, rank), jnp.float32),
            pltpu.VMEM((rank, n * T), bf),
            pltpu.VMEM((width, n * T), bf),
            pltpu.VMEM((rank, width), jnp.float32),
            pltpu.VMEM((rank, width), jnp.float32),
            pltpu.VMEM((Z, width, rank), bf),
            pltpu.VMEM((Y * CORES, Z, rows, width), bf),
            dma((5,)),
            dma((2, rank // 128)),
            dma((7 + Y, Z)),
            dma((7 + Y, Z)),
            dma((n,)),
            dma((n,)),
            dma((Y * CORES, Z)),
            dma((Y * CORES, Z)),
            dma((6, Z)),
        ],
        compiler_params=pltpu.CompilerParams(
            collective_id=0, has_side_effects=True, vmem_limit_bytes=60 * 2**20
        ),
        cost_estimate=pl.CostEstimate(
            flops=2 * T * rank * (D + n * width) + 2 * rank * rows * n * width,
            bytes_accessed=4 * D * rank, transcendentals=rank * width,
        ),
    )(tokens, ct, basis, moment, second_moment)
    update = jnp.transpose(out, (1, 0, 2)).reshape(rows, n * width)
    return (update, moment_next, second_next)


def solution(mesh):
    n = mesh.shape["rep"]
    Y = max(1, 4 // mesh.shape["groups"])
    Z = n // (Y * CORES)
    in_specs = (
        P(("groups", "rep"), None),
        P(("groups", "rep"), None),
        P("rep", None),
        P(None, "rep"),
        P(None, "rep"),
    )
    out_specs = (P(("groups", "rep"), None), P("groups", "rep"), P("groups", "rep"))
    return jax.shard_map(
        functools.partial(on_device, n, Z, Y),
        mesh=mesh, in_specs=in_specs, out_specs=out_specs, check_vma=False,
    )
```

time: 353 us -> 308 us (0.87)
  Pallas kernels: 0 us -> 274 us
  blocking collectives: 219 us -> 0 us
  waiting for transfers between devices: 80.4 us -> 0 us
  matrix products: 25.5 us -> 0 us
  local copies, waits for them, and re-layouts: 13.2 us -> 33.1 us
  between operations: 14.1 us -> 0.65 us
    pallas_call x0 -> x1, Pallas kernels: none -> 274 us  [on_device(): pl.pallas_call(functools.partial(kernel, n, Z, Y), out_shape=(jax.ShapeDt...]
    all_to_all x2 -> x0, blocking collectives: 219 us -> none  [the longest x1 128 us: on_device(): lax.all_to_all(update_columns, 'rep', split_axis=0, concat_axis=1, tiled=...]
    all_gather x2 -> x0, waiting for transfers between devices: 79.7 us -> none  [the longest x1 79.7 us: on_device(): full_basis = lax.all_gather(basis, 'rep', axis=0, tiled=True)]
    dot_general x3 -> x0, matrix products: 25.5 us -> none  [the longest x1 12 us: on_device(): expanded = jnp.dot(full_basis, ratio, preferred_element_type=jnp.float32)]
    transpose x0 -> x2, local copies, waits for them, and re-layouts: none -> 13.1 us  [the longest x1 8.43 us: on_device(): update = jnp.transpose(out, (1, 0, 2)).reshape(rows, n * width)]
    unnamed x8 -> x9, local copies, waits for them, and re-layouts: 12.8 us -> 20 us
  transfers between devices with their start and end apart: 2 -> 0, of which waited for: 1 -> 0; matrix products, arithmetic and copies ran while one was open for 1% -> 0% of each run, Pallas kernels for 0% -> 0%
where the time goes in v1:
time: 308 us
  Pallas kernels  274 us (89%)
  local copies, waits for them, and re-layouts  33.1 us (11%)
    pallas_call x1, Pallas kernels, on_device(): pl.pallas_call(functools.partial(kernel, n, Z, Y), out_shape=(jax.ShapeDt...  274 us
    unnamed x9, local copies, waits for them, and re-layouts  20 us
    transpose x1, local copies, waits for them, and re-layouts, on_device(): update = jnp.transpose(out, (1, 0, 2)).reshape(rows, n * width)  8.43 us

profile of v1, /device:TPU:1, one launch (start us, length us, event | category | flops | bytes accessed | tf_op | source)
XLA Modules:
  0.0 307.9 jit_solution(13902232300933210865)
XLA Ops:
  0.6 0.0 copy-start.1
  0.6 4.7 %copy.13 = bf16[11008,128]{1,0:T(8,128)(2,1)} copy(bf16[11008,128]{0,1:T(8,128)(2,1)} %bitcast.6) | data formatting | bytes 5636096 | tf_op jit(solution)/shard_map/transpose | solution.py:291
  5.3 0.0 copy-done.1
  5.3 2.3 copy.14.moment_hbm
  7.6 3.5 %copy.15.second_hbm = f32[1024,688]{1,0:T(8,128)} copy(f32[1024,688]{0,1:T(8,128)} %param.9) | data formatting | bytes 5636096 | tf_op args[4]
  11.2 274.2 %shard_map.76 = (bf16[16,256,688]{2,1,0:T(8,128)(2,1)}, f32[1024,688]{1,0:T(8,128)}, f32[1024,688]{1,0:T(8,128)}) custom-call(bf16[128,4096]{1,0:T(8,128)(2,1)} %tokens_hbm.1, bf16[16,688,128]{2,1,0:T(8,128)(2,1)} %bitcast.7, bf16[256,1024]{1,0:T(8,128)(2,1)} %basis_hbm.1, f32[1024,688]{1,0:T(8,128)} %copy.14.moment_hbm, f32[1024,688]{1,0:T(8,128)} %copy.15.second_hbm), custom_call_target="tpu_custom_call" | custom-call | flops 9730785280 | bytes 16777216 | tf_op jit(solution)/shard_map/pallas_call | solution.py:294
  285.4 8.4 %copy.16 = bf16[256,16,688]{0,2,1:T(8,128)(2,1)} copy(bf16[256,16,688]{2,0,1:T(8,128)(2,1)} %bitcast.5) | data formatting | bytes 11272192 | tf_op jit(solution)/shard_map/transpose | solution.py:331
  293.8 8.3 %copy.17 = bf16[256,11008]{1,0:T(8,128)(2,1)} copy(bf16[256,11008]{0,1:T(8,128)(2,1)} %bitcast.4) | data formatting | bytes 11272192
  302.1 0.0 copy-start
  302.1 3.6 %copy.18 = f32[1024,688]{0,1:T(8,128)} copy(f32[1024,688]{1,0:T(8,128)} %get-tuple-element.13) | data formatting | bytes 5636096
  305.7 0.0 copy-done
  305.7 2.2 copy.19
Async XLA Ops:
  0.6 4.7 %copy-start.1 = (f32[1024,688]{0,1:T(8,128)S(1)}, f32[1024,688]{0,1:T(8,128)}, u32[]{:S(2)}) copy-start(f32[1024,688]{0,1:T(8,128)} %param.8) | copy-start | bytes 8454148
  302.1 3.6 %copy-start = (f32[1024,688]{1,0:T(8,128)S(1)}, f32[1024,688]{1,0:T(8,128)}, u32[]{:S(2)}) copy-start(f32[1024,688]{1,0:T(8,128)} %get-tuple-element.14) | copy-start | bytes 8454148

commit v2 on v1

v2 whole, which is shorter than its diff:
```python
import functools

import jax
import jax.numpy as jnp
from jax import lax
from jax.experimental import pallas as pl
from jax.experimental.pallas import tpu as pltpu
from jax.sharding import PartitionSpec as P

CORES = 2
NT = (((1,), (1,)), ((), ()))


def parts_of(width):
    if width % 16:
        return ((0, width),)
    half = (width // 2 + 15) // 16 * 16
    return ((0, half), (half, width - half))


def kernel(
    n, Z, Y, tokens_hbm, ct_hbm, basis_hbm, moment_hbm, second_hbm,
    out_hbm, moment_out, second_out,
    tok, ball, pacc, ptall, ctall, mom, sec, rt, ubuf,
    lsem, asem, bsem, psem, csem_s, csem_r, usem_s, usem_r, rsem,
):
    me = lax.axis_index("rep")
    z = me // (Y * CORES)
    y = (me // CORES) % Y
    c = me % CORES
    rows = basis_hbm.shape[0]
    T = tokens_hbm.shape[0]
    rank = basis_hbm.shape[1]
    parts = parts_of(moment_hbm.shape[0])
    R = len(parts)

    def dev(zz, yy, cc):
        return (zz * Y + yy) * CORES + cc

    barrier = pltpu.get_barrier_semaphore()

    @pl.loop(1, n)
    def _(k):
        pl.semaphore_signal(
            barrier, inc=1, device_id={"rep": (me + k) % n},
            device_id_type=pl.DeviceIdType.MESH,
        )

    def local(src, dst, i):
        return pltpu.make_async_copy(src, dst, lsem.at[i])

    def remote(src, dst, ss, rs, to):
        return pltpu.make_async_remote_copy(
            src_ref=src, dst_ref=dst, send_sem=ss, recv_sem=rs,
            device_id={"rep": to}, device_id_type=pl.DeviceIdType.MESH,
        )

    def bas(b):
        return ball.at[pl.ds(pl.multiple_of(b * rows, 16), rows), :]

    def pro(b):
        return ptall.at[pl.ds(pl.multiple_of(b * T, 128), T), :]

    def cot(b):
        return ctall.at[:, pl.ds(pl.multiple_of(b * T, 128), T)]

    own = local(basis_hbm, bas(me), 0)
    own.start()
    load_tok = local(tokens_hbm, tok, 1)
    load_tok.start()
    load_mom = local(moment_hbm, mom, 2)
    load_mom.start()
    load_sec = local(second_hbm, sec, 3)
    load_sec.start()
    own_ct = local(ct_hbm.at[me], cot(me), 4)
    own_ct.start()
    own.wait()
    pl.semaphore_wait(barrier, n - 1)

    def up(blk, S, zs, *j):
        b = blk(dev(zs, y, c), *j)
        i = zs * R + j[0] if j else zs
        return remote(b, b, S.at[0, i], S.at[5, i], dev((z + 1) % Z, y, c))

    def down(blk, S, zs, *j):
        b = blk(dev(zs, y, c), *j)
        i = zs * R + j[0] if j else zs
        return remote(b, b, S.at[1, i], S.at[5, i], dev((z + Z - 1) % Z, y, c))

    def across(blk, S, zs, recv=False):
        b = blk(dev(zs, (y + 1) % Y if recv else y, c))
        return remote(b, b, S.at[2, zs], S.at[6, zs], dev(z, (y + 1) % Y, c))

    def core(blk, S, zs, ys, recv=False):
        b = blk(dev(zs, ys, (c + 1) % CORES if recv else c))
        i = (ys + Y - y) % Y
        return remote(b, b, S.at[3 + i, zs], S.at[7 + ys, zs], dev(z, y, (c + 1) % CORES))

    def spread(blk, S, zs):
        if Y > 1:
            across(blk, S, zs).start()
        core(blk, S, zs, y).start()

    def both(k, f):
        @pl.when(z - k >= 0)
        def _():
            f(z - k, True)

        @pl.when(z + k < Z)
        def _():
            f(z + k, False)

    def line_start(blk, S, *j):
        @pl.when(z + 1 < Z)
        def _():
            up(blk, S, z, *j).start()

        @pl.when(z >= 1)
        def _():
            down(blk, S, z, *j).start()

    def line_take(blk, S, zs, below, *j):
        up(blk, S, zs, *j).wait_recv()
        if below:
            @pl.when(z + 1 < Z)
            def _():
                up(blk, S, zs, *j).start()
        else:
            @pl.when(z >= 1)
            def _():
                down(blk, S, zs, *j).start()

    def line_sent(blk, S, *j):
        @pl.loop(0, Z)
        def _(zs):
            @pl.when((zs <= z) & (z + 1 < Z))
            def _():
                up(blk, S, zs, *j).wait_send()

            @pl.when((zs >= z) & (z >= 1))
            def _():
                down(blk, S, zs, *j).wait_send()

    def gather(blk, S, middle=None):
        def crossed(zs, _=None):
            if Y > 1:
                across(blk, S, zs, recv=True).wait_recv()
                core(blk, S, zs, (y + 1) % Y).start()

        def arrived(zs, below):
            line_take(blk, S, zs, below)
            spread(blk, S, zs)

        line_start(blk, S)
        spread(blk, S, z)

        @pl.loop(1, Z)
        def _(k):
            both(k, arrived)

        if middle is not None:
            middle()
        crossed(z)

        @pl.loop(1, Z)
        def _(k):
            both(k, crossed)

        @pl.loop(0, Z)
        def _(zs):
            for ys in range(Y):
                core(blk, S, zs, ys, recv=True).wait_recv()

    def gather_sent(blk, S):
        line_sent(blk, S)

        @pl.loop(0, Z)
        def _(zs):
            if Y > 1:
                across(blk, S, zs).wait_send()
            for ys in range(Y):
                core(blk, S, zs, ys).wait_send()

    def cot_copy(k):
        to = (me + k) % n
        return remote(ct_hbm.at[to], cot(me), csem_s.at[k], csem_r.at[me], to)

    def cot_start():
        @pl.loop(1, n)
        def _(k):
            cot_copy(k).start()

    gather(bas, bsem, cot_start)

    load_tok.wait()
    pacc[...] = jnp.zeros_like(pacc)
    step = 512

    @pl.loop(0, ball.shape[0] // step)
    def _(k):
        at = pl.ds(pl.multiple_of(k * step, step), step)
        pacc[...] += jnp.dot(tok[:, at], ball[at, :], preferred_element_type=jnp.float32)

    pro(me)[...] = pacc[...].astype(jnp.bfloat16)
    gather(pro, psem)

    @pl.loop(1, n)
    def _(k):
        src = (me + k) % n
        remote(cot(src), cot(src), csem_s.at[k], csem_r.at[src], src).wait_recv()

    own_ct.wait()
    load_mom.wait()
    load_sec.wait()

    def adam_copy(i, j):
        src, dst = ((mom, moment_out), (sec, second_out))[i]
        at = pl.ds(*parts[j])
        return pltpu.make_async_copy(src.at[at, :], dst.at[at, :], asem.at[i, j])

    def rat(b, j):
        return rt.at[b // (Y * CORES), pl.ds(*parts[j]), :]

    planes = Y * CORES

    def u_copy(p, zs, j, recv=False):
        at = pl.ds(*parts[j])
        b = dev(zs, 0, 0) + (p if recv else me % planes)
        i = zs * R + j
        return remote(
            ubuf.at[p, zs, at, :], out_hbm.at[b, at, :], usem_s.at[p, i],
            usem_r.at[p if recv else me % planes, i], z * planes + p,
        )

    def u_local(zs, j):
        at = pl.ds(*parts[j])
        q = me % planes
        return pltpu.make_async_copy(
            ubuf.at[q, zs, at, :], out_hbm.at[dev(zs, y, c), at, :], usem_s.at[q, zs * R + j]
        )

    def expand(zs, j):
        part = pl.ds(*parts[j])
        for i in (1, 2, 0, 3) if planes == 4 else range(planes):
            p = (me + i + 1) % planes
            at = pl.ds(pl.multiple_of((z * planes + p) * rows, 16), rows)
            ubuf[p, zs, part, :] = lax.dot_general(
                rt[zs, part, :], ball[at, :], NT, preferred_element_type=jnp.float32
            ).astype(jnp.bfloat16)
            if i < planes - 1:
                u_copy(p, zs, j).start()
            else:
                u_local(zs, j).start()

    for j in range(R):
        at = pl.ds(*parts[j])
        low = jnp.dot(ctall[at, :], ptall[...], preferred_element_type=jnp.float32)
        moment_next = 0.9 * mom[at, :] + 0.1 * low
        second_next = 0.999 * sec[at, :] + 0.001 * low * low
        mom[at, :] = moment_next
        sec[at, :] = second_next
        ratio = moment_next / (jnp.sqrt(second_next) + 1e-08)
        rt[z, at, :] = ratio.astype(jnp.bfloat16)
        line_start(rat, rsem, j)
        adam_copy(0, j).start()
        adam_copy(1, j).start()

    for j in range(R):
        expand(z, j)

    @pl.loop(1, Z)
    def _(k):
        for j in range(R):
            both(k, lambda zs, below: line_take(rat, rsem, zs, below, j))
            both(k, lambda zs, below: expand(zs, j))

    gather_sent(bas, bsem)
    gather_sent(pro, psem)
    for j in range(R):
        line_sent(rat, rsem, j)

    @pl.loop(1, n)
    def _(k):
        cot_copy(k).wait_send()

    for j in range(R):
        adam_copy(0, j).wait()
        adam_copy(1, j).wait()

    @pl.loop(0, Z)
    def _(zs):
        for j in range(R):
            for i in range(1, planes):
                p = (me + i) % planes
                u_copy(p, zs, j).wait_send()
                u_copy(p, zs, j, recv=True).wait_recv()
            u_local(zs, j).wait()


def on_device(n, Z, Y, tokens, cotangent, basis, moment, second_moment):
    T, D = tokens.shape
    rows, rank = basis.shape
    width = moment.shape[1]
    R = len(parts_of(width))
    bf = jnp.bfloat16
    ct = cotangent.T.reshape(n, width, T)
    any_spec = pl.BlockSpec(memory_space=pl.ANY)
    dma = pltpu.SemaphoreType.DMA
    out, moment_next, second_next = pl.pallas_call(
        functools.partial(kernel, n, Z, Y),
        out_shape=(
            jax.ShapeDtypeStruct((n, width, rows), bf),
            jax.ShapeDtypeStruct((width, rank), jnp.float32),
            jax.ShapeDtypeStruct((width, rank), jnp.float32),
        ),
        in_specs=[any_spec] * 5,
        out_specs=(any_spec,) * 3,
        scratch_shapes=[
            pltpu.VMEM((T, D), bf),
            pltpu.VMEM((D, rank), bf),
            pltpu.VMEM((T, rank), jnp.float32),
            pltpu.VMEM((n * T, rank), bf),
            pltpu.VMEM((width, n * T), bf),
            pltpu.VMEM((width, rank), jnp.float32),
            pltpu.VMEM((width, rank), jnp.float32),
            pltpu.VMEM((Z, width, rank), bf),
            pltpu.VMEM((Y * CORES, Z, width, rows), bf),
            dma((5,)),
            dma((2, R)),
            dma((7 + Y, Z)),
            dma((7 + Y, Z)),
            dma((n,)),
            dma((n,)),
            dma((Y * CORES, Z * R)),
            dma((Y * CORES, Z * R)),
            dma((6, Z * R)),
        ],
        compiler_params=pltpu.CompilerParams(
            collective_id=0, has_side_effects=True, vmem_limit_bytes=60 * 2**20
        ),
        cost_estimate=pl.CostEstimate(
            flops=2 * T * rank * (D + n * width) + 2 * rank * rows * n * width,
            bytes_accessed=4 * D * rank, transcendentals=rank * width,
        ),
    )(tokens, ct, basis, moment.T, second_moment.T)
    update = out.reshape(n * width, rows).T
    return (update, moment_next.T, second_next.T)


def solution(mesh):
    n = mesh.shape["rep"]
    Y = max(1, 4 // mesh.shape["groups"])
    Z = n // (Y * CORES)
    in_specs = (
        P(("groups", "rep"), None),
        P(("groups", "rep"), None),
        P("rep", None),
        P(None, "rep"),
        P(None, "rep"),
    )
    out_specs = (P(("groups", "rep"), None), P("groups", "rep"), P("groups", "rep"))
    return jax.shard_map(
        functools.partial(on_device, n, Z, Y),
        mesh=mesh, in_specs=in_specs, out_specs=out_specs, check_vma=False,
    )
```

time: 308 us -> 263 us (0.85)
  Pallas kernels: 274 us -> 245 us
  local copies, waits for them, and re-layouts: 33.1 us -> 17.3 us
    pallas_call x1, Pallas kernels: 274 us -> 245 us  [on_device(): pl.pallas_call(functools.partial(kernel, n, Z, Y), out_shape=(jax.ShapeDt...]
    unnamed x9 -> x6, local copies, waits for them, and re-layouts: 20 us -> 4.37 us
    reshape x0 -> x1, local copies, waits for them, and re-layouts: none -> 8.47 us  [on_device(): update = out.reshape(n * width, rows).T]
    transpose x1 -> x0, local copies, waits for them, and re-layouts: 8.43 us -> none  [on_device(): update = jnp.transpose(out, (1, 0, 2)).reshape(rows, n * width)]
where the time goes in v2:
time: 263 us
  Pallas kernels  245 us (93%)
  local copies, waits for them, and re-layouts  17.3 us (7%)
    pallas_call x1, Pallas kernels, on_device(): pl.pallas_call(functools.partial(kernel, n, Z, Y), out_shape=(jax.ShapeDt...  245 us
    reshape x1, local copies, waits for them, and re-layouts, on_device(): update = out.reshape(n * width, rows).T  8.47 us

profile of v2, /device:TPU:1, one launch (start us, length us, event | category | flops | bytes accessed | tf_op | source)
XLA Modules:
  0.0 262.6 jit_solution(11299186154753095540)
XLA Ops:
  0.6 4.5 %copy.8 = bf16[11008,128]{1,0:T(8,128)(2,1)} copy(bf16[11008,128]{0,1:T(8,128)(2,1)} %bitcast.10) | data formatting | bytes 5636096 | tf_op jit(solution)/shard_map/transpose | solution.py:306
  5.1 244.6 %shard_map.76 = (bf16[16,688,256]{2,1,0:T(8,128)(2,1)}, f32[688,1024]{1,0:T(8,128)}, f32[688,1024]{1,0:T(8,128)}) custom-call(bf16[128,4096]{1,0:T(8,128)(2,1)} %tokens_hbm.1, bf16[16,688,128]{2,1,0:T(8,128)(2,1)} %bitcast.13, bf16[256,1024]{1,0:T(8,128)(2,1)} %basis_hbm.1, f32[688,1024]{1,0:T(8,128)} %bitcast.14, f32[688,1024]{1,0:T(8,128)} %bitcast.15), custom_call_target="tpu_custom_call" | custom-call | flops 9730785280 | bytes 16777216 | tf_op jit(solution)/shard_map/pallas_call | solution.py:309
  249.8 0.0 copy-start.1
  249.8 8.5 %copy.9 = bf16[11008,256]{0,1:T(8,128)(2,1)} copy(bf16[11008,256]{1,0:T(8,128)(2,1)} %bitcast.9) | data formatting | bytes 11272192 | tf_op jit(solution)/shard_map/reshape | solution.py:346
  258.2 0.0 copy-done.1
  258.2 0.0 copy-start
  258.2 1.6 copy.12
  259.8 1.3 copy-done
  261.1 1.6 copy.13
Async XLA Ops:
  249.8 8.5 %copy-start.1 = (f32[688,1024]{1,0:T(8,128)S(1)}, f32[688,1024]{1,0:T(8,128)}, u32[]{:S(2)}) copy-start(f32[688,1024]{1,0:T(8,128)} %get-tuple-element.7) | copy-start | bytes 8454148
  258.2 2.8 %copy-start = (f32[688,1024]{1,0:T(8,128)S(1)}, f32[688,1024]{1,0:T(8,128)}, u32[]{:S(2)}) copy-start(f32[688,1024]{1,0:T(8,128)} %get-tuple-element.8) | copy-start | bytes 8454148

commit v3 on v2

--- a/solution.py
+++ b/solution.py
@@ -8,20 +8,21 @@
 from jax.sharding import PartitionSpec as P
 
 CORES = 2
+BATCH = 2
 NT = (((1,), (1,)), ((), ()))
 
 
 def parts_of(width):
     if width % 16:
         return ((0, width),)
-    half = (width // 2 + 15) // 16 * 16
-    return ((0, half), (half, width - half))
+    part = (width // 4 + 15) // 16 * 16
+    return tuple((i * part, min(part, width - i * part)) for i in range(4))
 
 
 def kernel(
     n, Z, Y, tokens_hbm, ct_hbm, basis_hbm, moment_hbm, second_hbm,
     out_hbm, moment_out, second_out,
-    tok, ball, pacc, ptall, ctall, mom, sec, rt, ubuf,
+    tok, ball, pacc, ptall, ctall, mom, sec, rt, ubuf, cv, ctv,
     lsem, asem, bsem, psem, csem_s, csem_r, usem_s, usem_r, rsem,
 ):
     me = lax.axis_index("rep")
@@ -72,8 +73,19 @@
     load_mom.start()
     load_sec = local(second_hbm, sec, 3)
     load_sec.start()
-    own_ct = local(ct_hbm.at[me], cot(me), 4)
-    own_ct.start()
+    B = min(BATCH, (n - 1) // max(Z - 1, 1))
+    inside = ct_hbm.ndim == 2
+    width = moment_hbm.shape[0]
+
+    def ct_of(b):
+        return ctv.at[pl.ds(pl.multiple_of(b * width, 16), width), :] if inside else ct_hbm.at[b]
+
+    own_ct = local(ct_of(me), cot(me), 4)
+    if inside:
+        load_ct = local(ct_hbm, cv, 5)
+        load_ct.start()
+    else:
+        own_ct.start()
     own.wait()
     pl.semaphore_wait(barrier, n - 1)
 
@@ -141,7 +153,7 @@
             def _():
                 down(blk, S, zs, *j).wait_send()
 
-    def gather(blk, S, middle=None):
+    def gather(blk, S, early=None, middle=None, batch=None):
         def crossed(zs, _=None):
             if Y > 1:
                 across(blk, S, zs, recv=True).wait_recv()
@@ -153,10 +165,14 @@
 
         line_start(blk, S)
         spread(blk, S, z)
+        if early is not None:
+            early()
 
         @pl.loop(1, Z)
         def _(k):
             both(k, arrived)
+            if batch is not None:
+                batch(k)
 
         if middle is not None:
             middle()
@@ -183,14 +199,29 @@
 
     def cot_copy(k):
         to = (me + k) % n
-        return remote(ct_hbm.at[to], cot(me), csem_s.at[k], csem_r.at[me], to)
+        return remote(ct_of(to), cot(me), csem_s.at[k], csem_r.at[me], to)
 
     def cot_start():
-        @pl.loop(1, n)
+        @pl.loop(1 + (Z - 1) * B, n)
         def _(k):
             cot_copy(k).start()
 
-    gather(bas, bsem, cot_start)
+    def cot_batch(k):
+        for i in range(B):
+            cot_copy((k - 1) * B + i + 1).start()
+
+    def turn():
+        if inside:
+            load_ct.wait()
+
+            @pl.loop(0, cv.shape[1] // 128)
+            def _(k):
+                at = pl.ds(pl.multiple_of(k * 128, 128), 128)
+                ctv[at, :] = cv[:, at].T
+
+            own_ct.start()
+
+    gather(bas, bsem, turn, cot_start, cot_batch)
 
     load_tok.wait()
     pacc[...] = jnp.zeros_like(pacc)
@@ -303,7 +334,8 @@
     width = moment.shape[1]
     R = len(parts_of(width))
     bf = jnp.bfloat16
-    ct = cotangent.T.reshape(n, width, T)
+    inside = width % 16 == 0
+    ct = cotangent if inside else cotangent.T.reshape(n, width, T)
     any_spec = pl.BlockSpec(memory_space=pl.ANY)
     dma = pltpu.SemaphoreType.DMA
     out, moment_next, second_next = pl.pallas_call(
@@ -325,7 +357,9 @@
             pltpu.VMEM((width, rank), jnp.float32),
             pltpu.VMEM((Z, width, rank), bf),
             pltpu.VMEM((Y * CORES, Z, width, rows), bf),
-            dma((5,)),
+            pltpu.VMEM((T, n * width) if inside else (16, 128), bf),
+            pltpu.VMEM((n * width, T) if inside else (16, 128), bf),
+            dma((6,)),
             dma((2, R)),
             dma((7 + Y, Z)),
             dma((7 + Y, Z)),

time: 263 us -> 243 us (0.924)
  Pallas kernels: 245 us -> 229 us
  local copies, waits for them, and re-layouts: 17.3 us -> 12.8 us
    pallas_call x1, Pallas kernels: 245 us -> 229 us  [on_device(): pl.pallas_call(functools.partial(kernel, n, Z, Y), out_shape=(jax.ShapeDt...]
    transpose x1 -> x0, local copies, waits for them, and re-layouts: 4.5 us -> none  [on_device(): ct = cotangent.T.reshape(n, width, T)]
where the time goes in v3:
time: 243 us; the launch traced here: 242 us
  Pallas kernels  229 us (94%)
  local copies, waits for them, and re-layouts  12.8 us (5%)
    pallas_call x1, Pallas kernels, on_device(): pl.pallas_call(functools.partial(kernel, n, Z, Y), out_shape=(jax.ShapeDt...  229 us
    reshape x1, local copies, waits for them, and re-layouts, on_device(): update = out.reshape(n * width, rows).T  8.47 us

profile of v3, /device:TPU:1, one launch (start us, length us, event | category | flops | bytes accessed | tf_op | source)
XLA Modules:
  0.0 242.2 jit_solution(11829283096620155802)
XLA Ops:
  0.6 228.7 %shard_map.76 = (bf16[16,688,256]{2,1,0:T(8,128)(2,1)}, f32[688,1024]{1,0:T(8,128)}, f32[688,1024]{1,0:T(8,128)}) custom-call(bf16[128,4096]{1,0:T(8,128)(2,1)} %tokens_hbm.1, bf16[128,11008]{1,0:T(8,128)(2,1)} %ct_hbm.1, bf16[256,1024]{1,0:T(8,128)(2,1)} %basis_hbm.1, f32[688,1024]{1,0:T(8,128)} %bitcast.10, f32[688,1024]{1,0:T(8,128)} %bitcast.11), custom_call_target="tpu_custom_call" | custom-call | flops 9730785280 | bytes 16777216 | tf_op jit(solution)/shard_map/pallas_call | solution.py:341
  229.3 0.0 copy-start.1
  229.3 8.5 %copy.8 = bf16[11008,256]{0,1:T(8,128)(2,1)} copy(bf16[11008,256]{1,0:T(8,128)(2,1)} %bitcast.7) | data formatting | bytes 11272192 | tf_op jit(solution)/shard_map/reshape | solution.py:380
  237.8 0.0 copy-done.1
  237.8 0.0 copy-start
  237.8 1.6 copy.11
  239.4 1.3 copy-done
  240.6 1.6 copy.12
Async XLA Ops:
  229.3 8.5 %copy-start.1 = (f32[688,1024]{1,0:T(8,128)S(1)}, f32[688,1024]{1,0:T(8,128)}, u32[]{:S(2)}) copy-start(f32[688,1024]{1,0:T(8,128)} %get-tuple-element.7) | copy-start | bytes 8454148
  237.8 2.8 %copy-start = (f32[688,1024]{1,0:T(8,128)S(1)}, f32[688,1024]{1,0:T(8,128)}, u32[]{:S(2)}) copy-start(f32[688,1024]{1,0:T(8,128)} %get-tuple-element.8) | copy-start | bytes 8454148
